TPU v7x, 128 devices: a whole 4x4x4 slice. The times are simulated.
128 devices in a mesh: grp: 8 (over z, core), blk: 16 (over x, y).
Axes of the slice: x: 4, y: 4, z: 4, core: 2. Of those that a mesh axis runs over, the one named last changes fastest.
Arguments:
- left_tensor: bfloat16 [8, 3072, 768], P('grp', 'blk'), may hold values from -6 to 6
- right_tensor: bfloat16 [8, 768, 3072], P('grp', 'blk'), may hold values from -0.21875 to 0.21875
- diag_gate: float32 [8, 3072], P('grp'), may hold values from 0.2 to 1
- hop_gate: float32 [8, 3072], P('grp'), may hold values from -0.6 to 0.6
- sketch: bfloat16 [3072, 768], replicated, may hold values from -0.109375 to 0.109375
- sector_rows: int32 [8], P('grp'), may hold values from 1536 to 3072, as said below
- kept: int32 [8], P('grp'), may hold values from 384 to 768, as said below
Outputs:
- left_out: float32 [8, 3072, 768], P('grp', 'blk')
- right_out: float32 [3072, 8, 768], P('blk', 'grp')
Inputs may be any that keep to these rules, and one draw needn't show every extreme that they name: `sector_rows`: reached by some sector in every draw, at both ends. `kept`: reached by some sector in every draw, at both ends.
All inputs are finite; a program needn't handle non-finite values.
Results may differ from a plain program's by a relative error of at most 0.022.
Values may be sent and summed in bfloat16 or wider, within the bound.
A program may use at most 128 MiB of HBM per device.

v0:
```python
import math
import jax
import jax.numpy as jnp
from jax import lax
from jax.sharding import PartitionSpec as P


def padded_2(x, sides, width):
    for axis, dim in sides:
        size, length = (lax.axis_size(axis), x.shape[dim])
        up = [(i, (i + 1) % size) for i in range(size - 1)]
        down = [(j, i) for i, j in up]
        last = lax.slice_in_dim(x, length - width, length, axis=dim)
        initial = lax.slice_in_dim(x, 0, width, axis=dim)
        before = lax.ppermute(last, axis, up)
        after = lax.ppermute(initial, axis, down)
        x = jnp.concatenate([before, x, after], axis=dim)
    return x


def body(left_tensor, right_tensor, diag_gate, hop_gate, sketch, sector_rows, kept):
    sectors_here, rows_here, middle_states = left_tensor.shape
    kept_width = sketch.shape[1]
    blk_count = lax.axis_size("blk")
    total_rows = rows_here * blk_count
    theta_full = jnp.einsum(
        "srx,sxc->src",
        left_tensor,
        lax.all_gather(right_tensor, "blk", axis=1, tiled=True),
        preferred_element_type=jnp.float32,
    ).astype(jnp.bfloat16)
    padded = padded_2(theta_full, (("grp", 0),), 1).astype(jnp.float32)
    centre = padded[1:-1]
    mixed_wide = diag_gate[:, None, :] * centre + hop_gate[:, None, :] * (padded[:-2] + padded[2:])
    row_index = lax.axis_index("blk") * rows_here + jnp.arange(rows_here, dtype=jnp.int32)
    row_live = (row_index[None, :] < sector_rows[:, None]).astype(jnp.float32)
    mixed_b = (mixed_wide * row_live[:, :, None]).astype(jnp.bfloat16)
    col_live = (jnp.arange(kept_width, dtype=jnp.int32)[None, :] < kept[:, None]).astype(
        jnp.float32
    )
    sketched = jnp.einsum("src,ck->srk", mixed_b, sketch, preferred_element_type=jnp.float32)
    sketched = (sketched * col_live[:, None, :]).astype(jnp.bfloat16)
    gram_local = jnp.einsum("srk,srj->skj", sketched, sketched, preferred_element_type=jnp.float32)
    gram_mat = lax.psum(gram_local, "blk")
    gram_mat = (
        gram_mat + (1.0 - col_live)[:, :, None] * jnp.eye(kept_width, dtype=jnp.float32)[None]
    )
    factor = jnp.linalg.cholesky(gram_mat)
    sketch_wide = sketched.astype(jnp.float32)
    ortho_basis = lax.linalg.triangular_solve(
        factor, sketch_wide, left_side=False, lower=True, transpose_a=True
    )
    row_scale = math.sqrt(total_rows)
    left_out = ortho_basis * row_scale
    basis_b = ortho_basis.astype(jnp.bfloat16)
    summed = lax.psum_scatter(
        jnp.einsum("src,srk->csk", mixed_b, basis_b, preferred_element_type=jnp.float32).astype(
            jnp.bfloat16
        ),
        "blk",
        scatter_dimension=0,
        tiled=True,
    ).astype(jnp.float32)
    right_out = summed / row_scale
    return (left_out, right_out)


def solution(mesh):
    in_specs = (
        P("grp", "blk", None),
        P("grp", "blk", None),
        P("grp", None),
        P("grp", None),
        P(),
        P("grp"),
        P("grp"),
    )
    out_specs = (P("grp", "blk", None), P("blk", "grp", None))
    return jax.shard_map(body, mesh=mesh, in_specs=in_specs, out_specs=out_specs, check_vma=False)
```

profile of v0, /device:TPU:0, one launch (start us, length us, event | category | flops | bytes accessed | tf_op | source)
XLA Modules:
  0.0 565.9 jit_solution(544307361954773672)
XLA Ops:
  8.0 58.6 %all-gather.2.cloned.1.call-done = bf16[1,768,3072]{2,1,0:T(8,128)(2,1)} async-done(((bf16[1,48,3072]{2,1,0:T(8,128)(2,1)}), bf16[1,768,3072]{2,1,0:T(8,128)(2,1)}) %all-gather.2.cloned.1.call-update) | async-done | bytes 4718608 | tf_op jit(solution)/shard_map/all_gather | solution.py:29
  66.6 3.5 fusion.6
  74.6 3.5 collective-permute-done.1
  84.4 103.3 %all-reduce.3.cloned.1.call-done = f32[1,768,768]{1,2,0:T(8,128)} async-done(((f32[1,768,768]{1,2,0:T(8,128)}), f32[1,768,768]{1,2,0:T(8,128)}) %all-reduce.3.cloned.1.call-update) | async-done | bytes 2359312 | tf_op jit(solution)/shard_map/psum | solution.py:44
  187.7 3.2 select_add_fusion
  196.5 11.7 %custom-call.52 = f32[1,128,128]{2,1,0:T(8,128)S(1)} custom-call(f32[1,128,128]{2,1,0:T(8,128)S(1)} %cholesky.424), custom_call_target="Cholesky" | custom-call | tf_op jit(solution)/shard_map/jit(cholesky)/cholesky | solution.py:48
  208.2 9.8 %custom-call.53 = f32[1,1,128,128]{2,3,1,0:T(8,128)S(1)} custom-call(f32[1,1,128,128]{3,2,1,0:T(8,128)S(1)} %get-tuple-element.51), custom_call_target="InvertDiagBlocksLowerTriangular" | custom-call | tf_op jit(solution)/shard_map/jit(cholesky)/cholesky | solution.py:48
  221.2 11.7 %custom-call.54 = f32[1,128,128]{2,1,0:T(8,128)S(1)} custom-call(f32[1,128,128]{2,1,0:T(8,128)S(1)} %cholesky.428), custom_call_target="Cholesky" | custom-call | tf_op jit(solution)/shard_map/jit(cholesky)/cholesky | solution.py:48
  236.0 11.5 %custom-call.55 = f32[1,1,128,128]{2,3,1,0:T(8,128)} custom-call(f32[1,1,128,128]{3,2,1,0:T(8,128)} %get-tuple-element.49), custom_call_target="InvertDiagBlocksLowerTriangular" | custom-call | tf_op jit(solution)/shard_map/jit(cholesky)/cholesky | solution.py:48
  253.0 13.2 %custom-call.56 = f32[1,128,128]{2,1,0:T(8,128)} custom-call(f32[1,128,128]{2,1,0:T(8,128)} %cholesky.433), custom_call_target="Cholesky" | custom-call | tf_op jit(solution)/shard_map/jit(cholesky)/cholesky | solution.py:48
  270.1 11.3 %custom-call.57 = f32[1,1,128,128]{2,3,1,0:T(8,128)} custom-call(f32[1,1,128,128]{3,2,1,0:T(8,128)} %get-tuple-element.47), custom_call_target="InvertDiagBlocksLowerTriangular" | custom-call | tf_op jit(solution)/shard_map/jit(cholesky)/cholesky | solution.py:48
  286.1 13.6 %custom-call.58 = f32[1,128,128]{2,1,0:T(8,128)} custom-call(f32[1,128,128]{2,1,0:T(8,128)} %cholesky.438), custom_call_target="Cholesky" | custom-call | tf_op jit(solution)/shard_map/jit(cholesky)/cholesky | solution.py:48
  303.5 11.3 %custom-call.59 = f32[1,1,128,128]{2,3,1,0:T(8,128)} custom-call(f32[1,1,128,128]{3,2,1,0:T(8,128)} %get-tuple-element.45), custom_call_target="InvertDiagBlocksLowerTriangular" | custom-call | tf_op jit(solution)/shard_map/jit(cholesky)/cholesky | solution.py:48
  319.2 13.2 %custom-call.60 = f32[1,128,128]{2,1,0:T(8,128)} custom-call(f32[1,128,128]{2,1,0:T(8,128)} %cholesky.443), custom_call_target="Cholesky" | custom-call | tf_op jit(solution)/shard_map/jit(cholesky)/cholesky | solution.py:48
  336.8 11.3 %custom-call.61 = f32[1,1,128,128]{2,3,1,0:T(8,128)} custom-call(f32[1,1,128,128]{3,2,1,0:T(8,128)} %get-tuple-element.43), custom_call_target="InvertDiagBlocksLowerTriangular" | custom-call | tf_op jit(solution)/shard_map/jit(cholesky)/cholesky | solution.py:48
  349.2 2.3 fusion.34
  351.5 13.2 %custom-call.62 = f32[1,128,128]{2,1,0:T(8,128)} custom-call(f32[1,128,128]{2,1,0:T(8,128)} %fusion.34), custom_call_target="Cholesky" | custom-call | tf_op jit(solution)/shard_map/jit(cholesky)/cholesky | solution.py:48
  378.5 22.4 %while.1 = (s32[]{:T(128)}, f32[1,768,768]{1,2,0:T(8,128)}, s32[6,2]{0,1:T(2,128)S(1)}, f32[6,1,128,128]{3,2,1,0:T(8,128)}, s32[]{:T(128)}) while((s32[]{:T(128)}, f32[1,768,768]{1,2,0:T(8,128)}, s32[6,2]{0,1:T(2,128)S(1)}, f32[6,1,128,128]{3,2,1,0:T(8,128)}, s32[]{:T(128)}) %tuple.47), condition=%wide.while_cond, body=%wide.while_body.sunk | while | flops 2 | bytes 393833 | solution.py:50
  379.2 2.3 constant_dynamic-slice_fusion.5
  382.9 2.3 constant_dynamic-slice_fusion.5
  400.9 59.8 %custom-call.63 = f32[1,6,128,128]{2,3,1,0:T(8,128)S(1)} custom-call(f32[1,6,128,128]{3,2,1,0:T(8,128)} %bitcast.298), custom_call_target="InvertDiagBlocksLowerTriangular" | custom-call | tf_op jit(solution)/shard_map/triangular_solve | solution.py:50
  468.9 3.6 fusion.2
  472.5 6.6 %copy.46 = bf16[3072,768]{1,0:T(8,128)(2,1)} copy(bf16[3072,768]{0,1:T(8,128)(2,1)} %fusion.2) | data formatting | bytes 9437184
  480.0 76.8 %reduce-scatter.4.cloned.1.call-done = bf16[192,768]{1,0:T(8,128)(2,1)} async-done(((bf16[3072,768]{1,0:T(8,128)(2,1)}), bf16[192,768]{1,0:T(8,128)(2,1)}) %reduce-scatter.4.cloned.1.call-update) | async-done | bytes 294928
  (141 shorter events, 88.8 us)
Async XLA Ops:
  7.2 59.4 %copy-start = (bf16[1,192,768]{2,1,0:T(8,128)(2,1)S(1)}, bf16[1,192,768]{2,1,0:T(8,128)(2,1)}, u32[]{:S(2)}) copy-start(bf16[1,192,768]{2,1,0:T(8,128)(2,1)} %param.7) | copy-start | bytes 884740
  7.2 59.4 %all-gather.2.cloned.1.call-start = ((), (), s32[]{:S(2)}) async-start(), calls=%async_computation.1 | async-start | bytes 5013504 | tf_op jit(solution)/shard_map/all_gather | solution.py:29
  7.9 179.7 %all-reduce.3.cloned.1.call-start = ((), (), s32[]{:S(2)}) async-start(), calls=%async_computation.2 | async-start | bytes 4718592 | tf_op jit(solution)/shard_map/psum | solution.py:44
  66.6 14.1 %slice-start = ((s8[4718592]{0:T(1024)(128)(4,1)}), s8[524288]{0:T(1024)(128)(4,1)S(1)}, s32[]{:S(2)}) async-start(s8[4718592]{0:T(1024)(128)(4,1)} %bitcast.283), calls=%async_computation.4 | async-start | bytes 1048576
  70.1 4.5 collective-permute-start
  71.9 6.1 %collective-permute-start.1 = (bf16[1,192,3072]{2,1,0:T(8,128)(2,1)S(1)}, bf16[1,192,3072]{2,1,0:T(8,128)(2,1)}, u32[]{:S(2)}, u32[]{:S(2)}) collective-permute-start(bf16[1,192,3072]{2,1,0:T(8,128)(2,1)S(1)} %fusion.6), channel_id=1, source_target_pairs={{16,0},{32,16},{48,32},{64,48},{80,64},{96,80},{112,96},{17,1},{33... | collective-permute-start | bytes 3538952 | tf_op jit(solution)/shard_map/ppermute | solution.py:16
  74.5 5.3 copy-start.10
  74.5 5.3 copy-start.11
  74.5 6.2 %slice-start.1 = ((s8[4718592]{0:T(1024)(128)(4,1)}), s8[4194304]{0:T(1024)(128)(4,1)S(1)}, s32[]{:S(2)}) async-start(s8[4718592]{0:T(1024)(128)(4,1)} %bitcast.283), calls=%async_computation.5 | async-start | bytes 8388608
  80.7 1.1 copy-start.1
  83.8 473.0 %reduce-scatter.4.cloned.1.call-start = ((), (), s32[]{:S(2)}) async-start(), calls=%async_computation.3 | async-start | bytes 5013504
  195.1 1.4 copy-start.3
  219.6 14.6 %copy-start.4 = (f32[640,128]{0,1:T(8,128)}, f32[640,128]{0,1:T(8,128)S(1)}, u32[]{:S(2)}) copy-start(f32[640,128]{0,1:T(8,128)S(1)} %copy.26) | copy-start | bytes 983044
  221.1 13.1 %copy-start.6 = (f32[1,640,128]{2,1,0:T(8,128)}, f32[1,640,128]{2,1,0:T(8,128)S(1)}, u32[]{:S(2)}) copy-start(f32[1,640,128]{2,1,0:T(8,128)S(1)} %fusion.16) | copy-start | bytes 983044
  235.0 1.0 copy-start.5
  251.7 0.7 copy-start.7
  284.8 0.7 copy-start.8
  317.9 0.7 copy-start.9
  376.9 1.6 copy-start.12
  463.5 5.5 copy-start.2
Sparse Core Ops, SparseCore 0:
  10.2 56.3 all-gather.1
  83.9 103.6 all-reduce.2
  479.3 77.5 reduce-scatter.3
where the time goes:
time: 572 us; the launch traced here: 566 us
  waiting for transfers between devices  243 us (42%)
  other arithmetic  214 us (37%)
  local copies, waits for them, and re-layouts  51.9 us (9%)
  matrix products  34.4 us (6%)
  between operations  19.5 us (3%)
    another operation x22, other arithmetic, body(): factor = jnp.linalg.cholesky(gram_mat)  143 us
    psum x1, waiting for transfers between devices, body(): gram_mat = lax.psum(gram_local, 'blk')  103 us
    unnamed x4, waiting for transfers between devices  77.5 us
    another operation x3, other arithmetic, body(): lax.linalg.triangular_solve(factor, sketch_wide, left_side=False, lower=T...  61.9 us
    all_gather x1, waiting for transfers between devices, body(): lax.all_gather(right_tensor, 'blk', axis=1, tiled=True)  58.6 us
    another operation x30, local copies, waits for them, and re-layouts  22.3 us
    another operation x10, matrix products, body(): factor = jnp.linalg.cholesky(gram_mat)  16.2 us
    another operation x19, local copies, waits for them, and re-layouts, body(): factor = jnp.linalg.cholesky(gram_mat)  15 us
  transfers between devices with their start and end apart: 5, of which 4 were waited for; matrix products, arithmetic and copies ran while one was open for 0% of the time, Pallas kernels for 0%

commit v1 on v0

--- a/solution.py
+++ b/solution.py
@@ -41,7 +41,8 @@
     sketched = jnp.einsum("src,ck->srk", mixed_b, sketch, preferred_element_type=jnp.float32)
     sketched = (sketched * col_live[:, None, :]).astype(jnp.bfloat16)
     gram_local = jnp.einsum("srk,srj->skj", sketched, sketched, preferred_element_type=jnp.float32)
-    gram_mat = lax.psum(gram_local, "blk")
+    arr_next = jax.lax.all_gather(gram_local, axis_name="blk")
+    gram_mat = jnp.sum(arr_next, axis=0)
     gram_mat = (
         gram_mat + (1.0 - col_live)[:, :, None] * jnp.eye(kept_width, dtype=jnp.float32)[None]
     )

time: 572 us -> 690 us (1.21)
  waiting for transfers between devices: 243 us -> 371 us
  local copies, waits for them, and re-layouts: 51.9 us -> 43.5 us
    all_gather x0 -> x1, waiting for transfers between devices: none -> 231 us  [body(): arr_next = jax.lax.all_gather(gram_local, axis_name='blk')]
    psum x1 -> x0, waiting for transfers between devices: 103 us -> none  [body(): gram_mat = lax.psum(gram_local, 'blk')]
    reduce_sum x0 -> x1, other arithmetic: none -> 15.1 us  [body(): gram_mat = jnp.sum(arr_next, axis=0)]
    another operation x22, other arithmetic: 143 us -> 132 us  [body(): factor = jnp.linalg.cholesky(gram_mat)]
    another operation x19, local copies, waits for them, and re-layouts: 15 us -> 5.99 us  [body(): factor = jnp.linalg.cholesky(gram_mat)]
where the time goes in v1:
time: 690 us; the launch traced here: 684 us
  waiting for transfers between devices  371 us (54%)
  other arithmetic  215 us (31%)
  local copies, waits for them, and re-layouts  43.5 us (6%)
  matrix products  31.9 us (5%)
  between operations  19.6 us (3%)
    all_gather x1, waiting for transfers between devices, body(): arr_next = jax.lax.all_gather(gram_local, axis_name='blk')  231 us
    another operation x22, other arithmetic, body(): factor = jnp.linalg.cholesky(gram_mat)  132 us
    unnamed x4, waiting for transfers between devices  78.1 us
    another operation x3, other arithmetic, body(): lax.linalg.triangular_solve(factor, sketch_wide, left_side=False, lower=T...  61.3 us
    all_gather x1, waiting for transfers between devices, body(): lax.all_gather(right_tensor, 'blk', axis=1, tiled=True)  58.6 us
    another operation x30, local copies, waits for them, and re-layouts  21.1 us
    reduce_sum x1, other arithmetic, body(): gram_mat = jnp.sum(arr_next, axis=0)  15.1 us
  transfers between devices with their start and end apart: 5, of which 4 were waited for; matrix products, arithmetic and copies ran while one was open for 0% of the time, Pallas kernels for 0%

profile of v1, /device:TPU:0, one launch (start us, length us, event | category | flops | bytes accessed | tf_op | source)
XLA Modules:
  0.0 684.4 jit_solution(17125785260043376109)
XLA Ops:
  8.0 58.6 %all-gather.4.cloned.1.call-done = bf16[1,768,3072]{2,1,0:T(8,128)(2,1)} async-done(((bf16[1,48,3072]{2,1,0:T(8,128)(2,1)}), bf16[1,768,3072]{2,1,0:T(8,128)(2,1)}) %all-gather.4.cloned.1.call-update) | async-done | bytes 4718608 | tf_op jit(solution)/shard_map/all_gather | solution.py:29
  66.6 3.5 fusion.6
  74.6 3.5 collective-permute-done.1
  83.9 230.8 %all-gather.6.cloned.1.call-done = f32[12288,768]{1,0:T(8,128)} async-done(((f32[768,768]{1,0:T(8,128)}), f32[12288,768]{1,0:T(8,128)}) %all-gather.6.cloned.1.call-update) | async-done | bytes 37748752 | tf_op jit(solution)/shard_map/all_gather | solution.py:44
  314.7 15.1 %reduce.55 = f32[768,768]{1,0:T(8,128)} reduce(f32[16,768,768]{2,1,0:T(8,128)} %bitcast.286, f32[]{:T(128)} %constant.244.clone.1), dimensions={0}, to_apply=%region_0.0 | reduce | flops 8847360 | bytes 40108036 | tf_op jit(solution)/shard_map/reduce_sum | solution.py:45
  333.4 3.2 copy.24
  340.0 11.7 %custom-call.52 = f32[1,128,128]{2,1,0:T(8,128)S(1)} custom-call(f32[1,128,128]{2,1,0:T(8,128)S(1)} %cholesky.424), custom_call_target="Cholesky" | custom-call | tf_op jit(solution)/shard_map/jit(cholesky)/cholesky | solution.py:49
  351.7 9.8 %custom-call.53 = f32[1,1,128,128]{2,3,1,0:T(8,128)S(1)} custom-call(f32[1,1,128,128]{3,2,1,0:T(8,128)S(1)} %get-tuple-element.51), custom_call_target="InvertDiagBlocksLowerTriangular" | custom-call | tf_op jit(solution)/shard_map/jit(cholesky)/cholesky | solution.py:49
  364.6 11.7 %custom-call.54 = f32[1,128,128]{2,1,0:T(8,128)S(1)} custom-call(f32[1,128,128]{2,1,0:T(8,128)S(1)} %cholesky.428), custom_call_target="Cholesky" | custom-call | tf_op jit(solution)/shard_map/jit(cholesky)/cholesky | solution.py:49
  377.6 10.0 %custom-call.55 = f32[1,1,128,128]{2,3,1,0:T(8,128)S(1)} custom-call(f32[1,1,128,128]{3,2,1,0:T(8,128)S(1)} %get-tuple-element.49), custom_call_target="InvertDiagBlocksLowerTriangular" | custom-call | tf_op jit(solution)/shard_map/jit(cholesky)/cholesky | solution.py:49
  391.6 13.2 %custom-call.56 = f32[1,128,128]{2,1,0:T(8,128)} custom-call(f32[1,128,128]{2,1,0:T(8,128)} %cholesky.433), custom_call_target="Cholesky" | custom-call | tf_op jit(solution)/shard_map/jit(cholesky)/cholesky | solution.py:49
  408.6 11.3 %custom-call.57 = f32[1,1,128,128]{2,3,1,0:T(8,128)} custom-call(f32[1,1,128,128]{3,2,1,0:T(8,128)} %get-tuple-element.47), custom_call_target="InvertDiagBlocksLowerTriangular" | custom-call | tf_op jit(solution)/shard_map/jit(cholesky)/cholesky | solution.py:49
  423.9 12.9 %custom-call.58 = f32[1,128,128]{2,1,0:T(8,128)S(1)} custom-call(f32[1,128,128]{2,1,0:T(8,128)} %cholesky.438), custom_call_target="Cholesky" | custom-call | tf_op jit(solution)/shard_map/jit(cholesky)/cholesky | solution.py:49
  439.0 10.6 %custom-call.59 = f32[1,1,128,128]{2,3,1,0:T(8,128)S(1)} custom-call(f32[1,1,128,128]{3,2,1,0:T(8,128)} %get-tuple-element.45), custom_call_target="InvertDiagBlocksLowerTriangular" | custom-call | tf_op jit(solution)/shard_map/jit(cholesky)/cholesky | solution.py:49
  451.9 11.7 %custom-call.60 = f32[1,128,128]{2,1,0:T(8,128)S(1)} custom-call(f32[1,128,128]{2,1,0:T(8,128)S(1)} %cholesky.443), custom_call_target="Cholesky" | custom-call | tf_op jit(solution)/shard_map/jit(cholesky)/cholesky | solution.py:49
  464.4 10.6 %custom-call.61 = f32[1,1,128,128]{2,3,1,0:T(8,128)S(1)} custom-call(f32[1,1,128,128]{3,2,1,0:T(8,128)} %get-tuple-element.43), custom_call_target="InvertDiagBlocksLowerTriangular" | custom-call | tf_op jit(solution)/shard_map/jit(cholesky)/cholesky | solution.py:49
  477.1 11.7 %custom-call.62 = f32[1,128,128]{2,1,0:T(8,128)S(1)} custom-call(f32[1,128,128]{2,1,0:T(8,128)S(1)} %fusion.34), custom_call_target="Cholesky" | custom-call | tf_op jit(solution)/shard_map/jit(cholesky)/cholesky | solution.py:49
  497.7 21.2 %while.1 = (s32[]{:T(128)}, f32[1,768,768]{1,2,0:T(8,128)}, s32[6,2]{0,1:T(2,128)S(1)}, f32[6,1,128,128]{3,2,1,0:T(8,128)}, s32[]{:T(128)}) while((s32[]{:T(128)}, f32[1,768,768]{1,2,0:T(8,128)}, s32[6,2]{0,1:T(2,128)S(1)}, f32[6,1,128,128]{3,2,1,0:T(8,128)}, s32[]{:T(128)}) %tuple.47), condition=%wide.while_cond, body=%wide.while_body.sunk | while | flops 2 | bytes 393833 | solution.py:51
  501.8 2.2 constant_dynamic-slice_fusion.5
  505.3 2.2 constant_dynamic-slice_fusion.5
  518.8 59.8 %custom-call.63 = f32[1,6,128,128]{2,3,1,0:T(8,128)S(1)} custom-call(f32[1,6,128,128]{3,2,1,0:T(8,128)} %bitcast.302), custom_call_target="InvertDiagBlocksLowerTriangular" | custom-call | tf_op jit(solution)/shard_map/triangular_solve | solution.py:51
  586.9 3.6 fusion.2
  590.5 6.6 copy.44
  598.0 77.3 %reduce-scatter.4.cloned.1.call-done = bf16[192,768]{1,0:T(8,128)(2,1)} async-done(((bf16[3072,768]{1,0:T(8,128)(2,1)}), bf16[192,768]{1,0:T(8,128)(2,1)}) %reduce-scatter.4.cloned.1.call-update) | async-done | bytes 294928
  (137 shorter events, 73.0 us)
Async XLA Ops:
  7.2 59.4 %copy-start = (bf16[1,192,768]{2,1,0:T(8,128)(2,1)S(1)}, bf16[1,192,768]{2,1,0:T(8,128)(2,1)}, u32[]{:S(2)}) copy-start(bf16[1,192,768]{2,1,0:T(8,128)(2,1)} %param.7) | copy-start | bytes 884740
  7.2 59.4 %all-gather.4.cloned.1.call-start = ((), (), s32[]{:S(2)}) async-start(), calls=%async_computation.1 | async-start | bytes 5013504 | tf_op jit(solution)/shard_map/all_gather | solution.py:29
  7.9 306.7 %all-gather.6.cloned.1.call-start = ((), (), s32[]{:S(2)}) async-start(), calls=%async_computation.2 | async-start | bytes 40108032 | tf_op jit(solution)/shard_map/all_gather | solution.py:44
  66.6 14.1 %slice-start = ((s8[4718592]{0:T(1024)(128)(4,1)}), s8[524288]{0:T(1024)(128)(4,1)S(1)}, s32[]{:S(2)}) async-start(s8[4718592]{0:T(1024)(128)(4,1)} %bitcast.287), calls=%async_computation.4 | async-start | bytes 1048576
  70.1 4.5 collective-permute-start
  71.9 6.1 collective-permute-start.1
  74.5 5.3 copy-start.8
  74.5 5.3 copy-start.9
  74.6 6.2 slice-start.1
  80.7 1.1 copy-start.2
  83.8 591.5 %reduce-scatter.4.cloned.1.call-start = ((), (), s32[]{:S(2)}) async-start(), calls=%async_computation.3 | async-start | bytes 5013504
  338.6 1.4 copy-start.4
  363.1 13.4 %copy-start.5 = (f32[640,128]{0,1:T(8,128)}, f32[640,128]{0,1:T(8,128)S(1)}, u32[]{:S(2)}) copy-start(f32[640,128]{0,1:T(8,128)S(1)} %copy.25) | copy-start | bytes 983044
  364.6 11.9 %copy-start.7 = (f32[1,640,128]{2,1,0:T(8,128)}, f32[1,640,128]{2,1,0:T(8,128)S(1)}, u32[]{:S(2)}) copy-start(f32[1,640,128]{2,1,0:T(8,128)S(1)} %fusion.16) | copy-start | bytes 983044
  376.6 1.0 copy-start.6
  581.4 5.5 copy-start.3
  597.1 80.6 %copy-start.1 = (bf16[1,192,768]{2,1,0:T(8,128)(2,1)S(1)}, bf16[1,192,768]{2,1,0:T(8,128)(2,1)}, u32[]{:S(2)}) copy-start(bf16[1,192,768]{2,1,0:T(8,128)(2,1)} %param.7) | copy-start | bytes 884740
Sparse Core Ops, SparseCore 0:
  10.2 56.3 all-gather.3
  83.9 230.6 all-gather.5
  597.2 78.0 reduce-scatter.3
